TPU v7x, 128 devices: a whole 4x4x4 slice. The times are simulated.
128 devices in a mesh: section: 2 (over y_hi), dp: 32 (over z, x, core), tensor: 2 (over y_lo).
Axes of the slice: x: 4, y: 4 (y_hi: 2, y_lo: 2; y = y_hi * 2 + y_lo), z: 4, core: 2. Of those that a mesh axis runs over, the one named last changes fastest.
Arguments:
- layer_input: bfloat16 [2, 32, 256, 1024], P(None, 'dp'), may hold values from -6 to 6
- cotangent: bfloat16 [2, 32, 256, 1024], P(None, 'dp'), may hold values from -6 to 6
- order: int32 [2], replicated, may hold values from 0 to 1, each once
- ln1_scale: bfloat16 [2, 1024], P('section'), may hold values from 0.099609375 to 1.8984375
- ln1_bias: bfloat16 [2, 1024], P('section'), may hold values from -1.796875 to 1.796875
- ln2_scale: bfloat16 [2, 1024], P('section'), may hold values from 0.099609375 to 1.8984375
- ln2_bias: bfloat16 [2, 1024], P('section'), may hold values from -1.796875 to 1.796875
- qkv_weight: bfloat16 [2, 1024, 3, 1024], P('section', None, None, 'tensor'), may hold values from -0.1875 to 0.1875
- qkv_bias: bfloat16 [2, 3, 1024], P('section', None, 'tensor'), may hold values from -1.796875 to 1.796875
- out_weight: bfloat16 [2, 1024, 1024], P('section', 'tensor'), may hold values from -0.75 to 0.75
- out_bias: bfloat16 [2, 1024], P('section'), may hold values from -3 to 3
- up_weight: bfloat16 [2, 1024, 4096], P('section', None, 'tensor'), may hold values from -0.1875 to 0.1875
- up_bias: bfloat16 [2, 4096], P('section', 'tensor'), may hold values from -3 to 3
- down_weight: bfloat16 [2, 4096, 1024], P('section', 'tensor'), may hold values from -0.09375 to 0.09375
- down_bias: bfloat16 [2, 1024], P('section'), may hold values from -3 to 3
Outputs:
- layer_outputs: bfloat16 [2, 2, 32, 256, 1024], P('section', None, 'dp')
- input_grads: bfloat16 [2, 2, 32, 256, 1024], P('section', None, 'dp')
- ln1_scale_grad: float32 [2, 1024], P('section')
- ln1_bias_grad: float32 [2, 1024], P('section')
- ln2_scale_grad: float32 [2, 1024], P('section')
- ln2_bias_grad: float32 [2, 1024], P('section')
- qkv_weight_grad: float32 [2, 1024, 3, 1024], P('section', None, None, 'tensor')
- qkv_bias_grad: float32 [2, 3, 1024], P('section', None, 'tensor')
- out_weight_grad: float32 [2, 1024, 1024], P('section', 'tensor')
- out_bias_grad: float32 [2, 1024], P('section')
- up_weight_grad: float32 [2, 1024, 4096], P('section', None, 'tensor')
- up_bias_grad: float32 [2, 4096], P('section', 'tensor')
- down_weight_grad: float32 [2, 4096, 1024], P('section', 'tensor')
- down_bias_grad: float32 [2, 1024], P('section')
Inputs may be any that keep to these rules, and one draw needn't show every extreme that they name: order names each of the 2 micro-batches once.
All inputs are finite; a program needn't handle non-finite values.
Results may differ from a plain program's by a relative error of at most 0.023.
Values may be sent and summed in bfloat16 or wider, within the bound.
A program may use at most 192 MiB of HBM per device.

v0:
```python
import jax
import jax.numpy as jnp
from jax import lax
from jax.sharding import PartitionSpec as P

HD = 64
ROT = 16


EPSILON = 1e-05


def passed_along(value, axis, steps):
    count = lax.axis_size(axis)
    leading, last = (max(0, -steps), min(count, count - steps))
    return lax.ppermute(value, axis, [(source, source + steps) for source in range(leading, last)])


def rotary_tables(length):
    half_rot = ROT // 2
    frequency = 1.0 / 10000.0 ** (jnp.arange(half_rot, dtype=jnp.float32) * 2.0 / ROT)
    where_at = jnp.arange(length, dtype=jnp.float32)
    angles = where_at[:, None] * frequency[None, :]
    angles = jnp.concatenate([angles, angles], axis=-1)[:, None, :]
    return (jnp.cos(angles), jnp.sin(angles))


def rotate(vector, cos_table, sin_table):
    half_rot = ROT // 2
    leading = vector[..., :ROT]
    turned = jnp.concatenate([-leading[..., half_rot:], leading[..., :half_rot]], axis=-1)
    return jnp.concatenate([leading * cos_table + turned * sin_table, vector[..., ROT:]], axis=-1)


def unrotate(vector, cos_table, sin_table):
    half_rot = ROT // 2
    leading = vector[..., :ROT]
    weighted = leading * sin_table
    turned = jnp.concatenate([weighted[..., half_rot:], -weighted[..., :half_rot]], axis=-1)
    return jnp.concatenate([leading * cos_table + turned, vector[..., ROT:]], axis=-1)


def gelu_slope(hidden):
    cdf_part = 0.5 * (1.0 + lax.erf(hidden * 0.7071067811865476))
    dens_part = jnp.exp(-0.5 * hidden * hidden) * 0.3989422804014327
    return cdf_part + hidden * dens_part


def standardize(inputs):
    centered = inputs - jnp.mean(inputs, axis=-1, keepdims=True)
    inv_std = lax.rsqrt(jnp.mean(centered * centered, axis=-1, keepdims=True) + EPSILON)
    return (centered * inv_std, inv_std)


def causal_mask(length):
    return jnp.arange(length)[:, None] >= jnp.arange(length)[None, :]


def forward_local(inputs, params, cos_table, sin_table):
    (
        scale_one,
        shift_one,
        scale_two,
        shift_two,
        qkv_w,
        qkv_b,
        out_w,
        out_b,
        up_w,
        up_b,
        down_w,
        down_b,
    ) = params
    batch_size, length = (inputs.shape[0], inputs.shape[1])
    head_count = qkv_w.shape[2] // HD
    normed, inv_std = standardize(inputs)
    first_in = (normed * scale_one.astype(jnp.float32) + shift_one.astype(jnp.float32)).astype(
        jnp.bfloat16
    )
    second_in = (normed * scale_two.astype(jnp.float32) + shift_two.astype(jnp.float32)).astype(
        jnp.bfloat16
    )
    projected = jnp.einsum(
        "bsd,dtc->bstc", first_in, qkv_w, preferred_element_type=jnp.float32
    ) + qkv_b.astype(jnp.float32)
    projected = projected.reshape(batch_size, length, 3, head_count, HD)
    queries = (rotate(projected[:, :, 0], cos_table, sin_table) * HD ** (-0.5)).astype(jnp.bfloat16)
    key_vecs = rotate(projected[:, :, 1], cos_table, sin_table).astype(jnp.bfloat16)
    values = projected[:, :, 2].astype(jnp.bfloat16)
    scores = jnp.einsum("bqhe,bkhe->bhqk", queries, key_vecs, preferred_element_type=jnp.float32)
    scores = jnp.where(causal_mask(length), scores, -1e30)
    row_max = jnp.max(scores, axis=-1, keepdims=True)
    exp_scores = jnp.exp(scores - row_max)
    row_total = jnp.sum(exp_scores, axis=-1, keepdims=True)
    attn_probs = (exp_scores / row_total).astype(jnp.bfloat16)
    log_total = (row_max + jnp.log(row_total))[..., 0]
    context = jnp.einsum("bhqk,bkhe->bqhe", attn_probs, values, preferred_element_type=jnp.float32)
    context = context.astype(jnp.bfloat16).reshape(batch_size, length, head_count * HD)
    hidden = jnp.einsum(
        "bsd,df->bsf", second_in, up_w, preferred_element_type=jnp.float32
    ) + up_b.astype(jnp.float32)
    activated = jax.nn.gelu(hidden, approximate=False).astype(jnp.bfloat16)
    branch_sum = jnp.einsum("bsh,hd->bsd", context, out_w, preferred_element_type=jnp.float32)
    branch_sum = branch_sum + jnp.einsum(
        "bsf,fd->bsd", activated, down_w, preferred_element_type=jnp.float32
    )
    saved = (
        normed,
        inv_std,
        first_in,
        second_in,
        queries.reshape(batch_size, length, head_count * HD),
        key_vecs.reshape(batch_size, length, head_count * HD),
        values.reshape(batch_size, length, head_count * HD),
        log_total,
        context,
        hidden,
        activated,
    )
    return (branch_sum, saved)


def backward_local(upstream, saved, params, cos_table, sin_table):
    (
        normed,
        inv_std,
        first_in,
        second_in,
        queries,
        key_vecs,
        values,
        log_total,
        context,
        hidden,
        activated,
    ) = saved
    (
        scale_one,
        shift_one,
        scale_two,
        shift_two,
        qkv_w,
        qkv_b,
        out_w,
        out_b,
        up_w,
        up_b,
        down_w,
        down_b,
    ) = params
    batch_size, length = (upstream.shape[0], upstream.shape[1])
    head_count = qkv_w.shape[2] // HD
    d_bias_out = jnp.sum(upstream.astype(jnp.float32), axis=(0, 1))
    d_out_w = jnp.einsum("bsh,bsd->hd", context, upstream, preferred_element_type=jnp.float32)
    d_down_w = jnp.einsum("bsf,bsd->fd", activated, upstream, preferred_element_type=jnp.float32)
    d_context = jnp.einsum("bsd,hd->bsh", upstream, out_w, preferred_element_type=jnp.float32)
    d_context = d_context.astype(jnp.bfloat16).reshape(batch_size, length, head_count, HD)
    d_active = jnp.einsum("bsd,fd->bsf", upstream, down_w, preferred_element_type=jnp.float32)
    d_hidden = (d_active * gelu_slope(hidden)).astype(jnp.bfloat16)
    d_up_b = jnp.sum(d_hidden.astype(jnp.float32), axis=(0, 1))
    d_up_w = jnp.einsum("bsd,bsf->df", second_in, d_hidden, preferred_element_type=jnp.float32)
    d_second = jnp.einsum("bsf,df->bsd", d_hidden, up_w, preferred_element_type=jnp.float32)
    query_heads = queries.reshape(batch_size, length, head_count, HD)
    key_heads = key_vecs.reshape(batch_size, length, head_count, HD)
    value_heads = values.reshape(batch_size, length, head_count, HD)
    scores = jnp.einsum(
        "bqhe,bkhe->bhqk", query_heads, key_heads, preferred_element_type=jnp.float32
    )
    attn_probs = jnp.where(causal_mask(length), jnp.exp(scores - log_total[..., None]), 0.0)
    d_values = jnp.einsum(
        "bhqk,bqhe->bkhe",
        attn_probs.astype(jnp.bfloat16),
        d_context,
        preferred_element_type=jnp.float32,
    )
    d_probs = jnp.einsum(
        "bqhe,bkhe->bhqk", d_context, value_heads, preferred_element_type=jnp.float32
    )
    inner_sum = jnp.sum(d_probs * attn_probs, axis=-1, keepdims=True)
    d_scores = (attn_probs * (d_probs - inner_sum)).astype(jnp.bfloat16)
    d_queries = jnp.einsum(
        "bhqk,bkhe->bqhe", d_scores, key_heads, preferred_element_type=jnp.float32
    )
    d_keys = jnp.einsum(
        "bhqk,bqhe->bkhe", d_scores, query_heads, preferred_element_type=jnp.float32
    )
    d_projected = jnp.stack(
        [
            unrotate(d_queries * HD ** (-0.5), cos_table, sin_table),
            unrotate(d_keys, cos_table, sin_table),
            d_values,
        ],
        axis=2,
    )
    d_projected = d_projected.reshape(batch_size, length, 3, head_count * HD).astype(jnp.bfloat16)
    d_qkv_b = jnp.sum(d_projected.astype(jnp.float32), axis=(0, 1))
    d_qkv_w = jnp.einsum("bsd,bstc->dtc", first_in, d_projected, preferred_element_type=jnp.float32)
    d_first = jnp.einsum("bstc,dtc->bsd", d_projected, qkv_w, preferred_element_type=jnp.float32)
    return ((d_qkv_w, d_qkv_b, d_out_w, d_bias_out, d_up_w, d_up_b, d_down_w), (d_first, d_second))


def put_slot(stored, index, value, is_valid):
    previous = lax.dynamic_index_in_dim(stored, index, 0, keepdims=False)
    return lax.dynamic_update_index_in_dim(stored, jnp.where(is_valid, value, previous), index, 0)


def shards(
    layer_input,
    cotangent,
    order,
    ln1_scale,
    ln1_bias,
    ln2_scale,
    ln2_bias,
    qkv_weight,
    qkv_bias,
    out_weight,
    out_bias,
    up_weight,
    up_bias,
    down_weight,
    down_bias,
):
    section_count = lax.axis_size("section")
    section_index = lax.axis_index("section")
    params = tuple(
        (
            entry[0]
            for entry in (
                ln1_scale,
                ln1_bias,
                ln2_scale,
                ln2_bias,
                qkv_weight,
                qkv_bias,
                out_weight,
                out_bias,
                up_weight,
                up_bias,
                down_weight,
                down_bias,
            )
        )
    )
    micro_count = layer_input.shape[0]
    batch_size, length, width = (layer_input.shape[1], layer_input.shape[2], layer_input.shape[3])
    head_width = qkv_weight.shape[3]
    hidden_width = up_weight.shape[2]
    head_count = head_width // HD
    cos_table, sin_table = rotary_tables(length)
    tick_count = micro_count + section_count - 1
    bias_sum = params[7].astype(jnp.float32) + params[11].astype(jnp.float32)

    def forward_tick(tick, carry):
        arriving, stored, out_store = carry
        slot_index = tick - section_index
        is_valid = (slot_index >= 0) & (slot_index < micro_count)
        clipped = jnp.clip(slot_index, 0, micro_count - 1)
        chosen = order[clipped]
        first_input = lax.dynamic_index_in_dim(layer_input, chosen, 0, keepdims=False)
        current = jnp.where(section_index == 0, first_input, arriving)
        branch_sum, saved = forward_local(current.astype(jnp.float32), params, cos_table, sin_table)
        summed = lax.psum(branch_sum, "tensor")
        result = (current.astype(jnp.float32) + summed + bias_sum).astype(jnp.bfloat16)
        stored = tuple(
            (put_slot(entry, clipped, value, is_valid) for entry, value in zip(stored, saved))
        )
        out_store = put_slot(out_store, chosen, result, is_valid)
        arriving = passed_along(result, "section", 1)
        return (arriving, stored, out_store)

    stored = (
        jnp.zeros((micro_count, batch_size, length, width), jnp.float32),
        jnp.zeros((micro_count, batch_size, length, 1), jnp.float32),
        jnp.zeros((micro_count, batch_size, length, width), jnp.bfloat16),
        jnp.zeros((micro_count, batch_size, length, width), jnp.bfloat16),
        jnp.zeros((micro_count, batch_size, length, head_width), jnp.bfloat16),
        jnp.zeros((micro_count, batch_size, length, head_width), jnp.bfloat16),
        jnp.zeros((micro_count, batch_size, length, head_width), jnp.bfloat16),
        jnp.zeros((micro_count, batch_size, head_count, length), jnp.float32),
        jnp.zeros((micro_count, batch_size, length, head_width), jnp.bfloat16),
        jnp.zeros((micro_count, batch_size, length, hidden_width), jnp.float32),
        jnp.zeros((micro_count, batch_size, length, hidden_width), jnp.bfloat16),
    )
    empty_rows = jnp.zeros((batch_size, length, width), jnp.bfloat16)
    out_store = jnp.zeros((micro_count, batch_size, length, width), jnp.bfloat16)
    arriving, stored, out_store = lax.fori_loop(
        0, tick_count, forward_tick, (empty_rows, stored, out_store)
    )

    def backward_tick(tick, carry):
        arriving, totals, grad_store = carry
        slot_index = tick - (section_count - 1 - section_index)
        is_valid = (slot_index >= 0) & (slot_index < micro_count)
        clipped = jnp.clip(slot_index, 0, micro_count - 1)
        chosen = order[clipped]
        given = lax.dynamic_index_in_dim(cotangent, clipped, 0, keepdims=False)
        upstream = jnp.where(section_index == section_count - 1, given, arriving)
        saved = tuple(
            (lax.dynamic_index_in_dim(entry, clipped, 0, keepdims=False) for entry in stored)
        )
        layer_grads, (d_first, d_second) = backward_local(
            upstream, saved, params, cos_table, sin_table
        )
        d_first, d_second = (
            lax.psum(d_first.astype(jnp.bfloat16), "tensor").astype(jnp.float32),
            lax.psum(d_second.astype(jnp.bfloat16), "tensor").astype(jnp.float32),
        )
        normed, inv_std = (saved[0], saved[1])
        norm_part = (
            jnp.sum(d_first * normed, axis=(0, 1)),
            jnp.sum(d_first, axis=(0, 1)),
            jnp.sum(d_second * normed, axis=(0, 1)),
            jnp.sum(d_second, axis=(0, 1)),
        )
        d_normed = d_first * params[0].astype(jnp.float32) + d_second * params[2].astype(
            jnp.float32
        )
        centered_grad = (
            d_normed
            - jnp.mean(d_normed, axis=-1, keepdims=True)
            - normed * jnp.mean(d_normed * normed, axis=-1, keepdims=True)
        )
        to_send = (upstream.astype(jnp.float32) + inv_std * centered_grad).astype(jnp.bfloat16)
        tick_part = tuple(
            (jnp.where(is_valid, grad_part, 0.0) for grad_part in norm_part + layer_grads)
        )
        totals = tuple((running + increment for running, increment in zip(totals, tick_part)))
        grad_store = put_slot(grad_store, chosen, to_send, is_valid)
        arriving = passed_along(to_send, "section", -1)
        return (arriving, totals, grad_store)

    zero_grads = (
        jnp.zeros((width,), jnp.float32),
        jnp.zeros((width,), jnp.float32),
        jnp.zeros((width,), jnp.float32),
        jnp.zeros((width,), jnp.float32),
        jnp.zeros((width, 3, head_width), jnp.float32),
        jnp.zeros((3, head_width), jnp.float32),
        jnp.zeros((head_width, width), jnp.float32),
        jnp.zeros((width,), jnp.float32),
        jnp.zeros((width, hidden_width), jnp.float32),
        jnp.zeros((hidden_width,), jnp.float32),
        jnp.zeros((hidden_width, width), jnp.float32),
    )
    grad_store = jnp.zeros((micro_count, batch_size, length, width), jnp.bfloat16)
    arriving, totals, grad_store = lax.fori_loop(
        0, tick_count, backward_tick, (empty_rows, zero_grads, grad_store)
    )
    totals = (
        lax.psum(totals[0].astype(jnp.bfloat16), "dp").astype(jnp.float32),
        lax.psum(totals[1].astype(jnp.bfloat16), "dp").astype(jnp.float32),
        lax.psum(totals[2].astype(jnp.bfloat16), "dp").astype(jnp.float32),
        lax.psum(totals[3].astype(jnp.bfloat16), "dp").astype(jnp.float32),
        lax.psum(totals[4].astype(jnp.bfloat16), "dp").astype(jnp.float32),
        lax.psum(totals[5].astype(jnp.bfloat16), "dp").astype(jnp.float32),
        lax.psum(totals[6].astype(jnp.bfloat16), "dp").astype(jnp.float32),
        lax.psum(totals[7].astype(jnp.bfloat16), "dp").astype(jnp.float32),
        lax.psum(totals[8].astype(jnp.bfloat16), "dp").astype(jnp.float32),
        lax.psum(totals[9].astype(jnp.bfloat16), "dp").astype(jnp.float32),
        lax.psum(totals[10].astype(jnp.bfloat16), "dp").astype(jnp.float32),
    )
    return (
        out_store[None],
        grad_store[None],
        totals[0][None],
        totals[1][None],
        totals[2][None],
        totals[3][None],
        totals[4][None],
        totals[5][None],
        totals[6][None],
        totals[7][None],
        totals[8][None],
        totals[9][None],
        totals[10][None],
        totals[7][None],
    )


def solution(mesh):
    return jax.shard_map(
        shards,
        mesh=mesh,
        in_specs=(
            P(None, "dp", None, None),
            P(None, "dp", None, None),
            P(),
            P("section", None),
            P("section", None),
            P("section", None),
            P("section", None),
            P("section", None, None, "tensor"),
            P("section", None, "tensor"),
            P("section", "tensor", None),
            P("section", None),
            P("section", None, "tensor"),
            P("section", "tensor"),
            P("section", "tensor", None),
            P("section", None),
        ),
        out_specs=(
            P("section", None, "dp", None, None),
            P("section", None, "dp", None, None),
            P("section", None),
            P("section", None),
            P("section", None),
            P("section", None),
            P("section", None, None, "tensor"),
            P("section", None, "tensor"),
            P("section", "tensor", None),
            P("section", None),
            P("section", None, "tensor"),
            P("section", "tensor"),
            P("section", "tensor", None),
            P("section", None),
        ),
        check_vma=False,
    )
```

profile of v0, /device:TPU:1, one launch (start us, length us, event | category | flops | bytes accessed | tf_op | source)
XLA Modules:
  0.0 772.4 jit_solution(14856833488150216717)
XLA Ops:
  28.7 301.2 %while.78 = (s32[]{:T(128)}, bf16[1,256,1024]{2,1,0:T(8,128)(2,1)}, f32[2,1,256,1024]{3,2,1,0:T(8,128)}, f32[2,1,256,1]{2,3,1,0:T(1,128)}, bf16[2,1,256,1024]{3,...) while((s32[]{:T(128)}, bf16[1,256,1024]{2,1,0:T(8,128)(2,1)}, ...), condition=%wide.region_6.7_spmd, body=%wide.region_0.6_spmd.sunk | while | flops 3409584128 | bytes 141941424 | solution.py:287
  47.3 9.2 %bitcast_dynamic-update-slice_fusion.10 = (bf16[2,1,256,2048]{3,2,1,0:T(8,128)(2,1)}, bf16[256,2048]{1,0:T(8,128)(2,1)S(1)}, f32[256,2048]{1,0:T(8,128)}) fusion(bf16[2,1,256,2048]{3,2,1,0:T(8,128)(2,1)} %get-tuple-element.2404, s32[]{:T(128)S(6)} %min.21, bf16[1,1,256,2048]{3,2,1,0:T(8,128)(2,1)} %constant_dynamic-slice_fusion.24, pred[]{:T(512)S(6)} %and.21, ...), kind=kOutput, calls=%fused_computation.47.clone.1 | convolution fusion | flops 1110441984 | bytes 9979909 | tf_op jit(solution)/shard_map/while/body/eval_jaxpr/bsd,df->bsf/dot_general | solution.py:99
  72.2 38.4 %all-reduce.11.cloned.1.call-done = f32[1,256,1024]{2,1,0:T(8,128)} async-done(((f32[1,256,1024]{2,1,0:T(8,128)}), f32[1,256,1024]{2,1,0:T(8,128)}) %all-reduce.11.cloned.1.call-update) | async-done | bytes 1048592 | tf_op jit(solution)/shard_map/while/body/eval_jaxpr/psum | solution.py:263
  120.9 8.1 %collective-permute-done = bf16[1,256,1024]{2,1,0:T(8,128)(2,1)} collective-permute-done((bf16[1,256,1024]{2,1,0:T(8,128)(2,1)S(1)}, bf16[1,256,1024]{2,1,0:T(8,128)(2,1)}, u32[]{:S(2)}, u32[]{:S(2)}) %collective-permute-start) | collective-permute-done | bytes 524320 | tf_op jit(solution)/shard_map/while/body/eval_jaxpr/ppermute | solution.py:16
  147.7 9.2 %bitcast_dynamic-update-slice_fusion.10 = (bf16[2,1,256,2048]{3,2,1,0:T(8,128)(2,1)}, bf16[256,2048]{1,0:T(8,128)(2,1)S(1)}, f32[256,2048]{1,0:T(8,128)}) fusion(bf16[2,1,256,2048]{3,2,1,0:T(8,128)(2,1)} %get-tuple-element.2404, s32[]{:T(128)S(6)} %min.21, bf16[1,1,256,2048]{3,2,1,0:T(8,128)(2,1)} %constant_dynamic-slice_fusion.24, pred[]{:T(512)S(6)} %and.21, ...), kind=kOutput, calls=%fused_computation.47.clone.1 | convolution fusion | flops 1110441984 | bytes 9979909 | tf_op jit(solution)/shard_map/while/body/eval_jaxpr/bsd,df->bsf/dot_general | solution.py:99
  172.6 38.4 %all-reduce.11.cloned.1.call-done = f32[1,256,1024]{2,1,0:T(8,128)} async-done(((f32[1,256,1024]{2,1,0:T(8,128)}), f32[1,256,1024]{2,1,0:T(8,128)}) %all-reduce.11.cloned.1.call-update) | async-done | bytes 1048592 | tf_op jit(solution)/shard_map/while/body/eval_jaxpr/psum | solution.py:263
  221.4 8.1 %collective-permute-done = bf16[1,256,1024]{2,1,0:T(8,128)(2,1)} collective-permute-done((bf16[1,256,1024]{2,1,0:T(8,128)(2,1)S(1)}, bf16[1,256,1024]{2,1,0:T(8,128)(2,1)}, u32[]{:S(2)}, u32[]{:S(2)}) %collective-permute-start) | collective-permute-done | bytes 524320 | tf_op jit(solution)/shard_map/while/body/eval_jaxpr/ppermute | solution.py:16
  248.1 9.2 %bitcast_dynamic-update-slice_fusion.10 = (bf16[2,1,256,2048]{3,2,1,0:T(8,128)(2,1)}, bf16[256,2048]{1,0:T(8,128)(2,1)S(1)}, f32[256,2048]{1,0:T(8,128)}) fusion(bf16[2,1,256,2048]{3,2,1,0:T(8,128)(2,1)} %get-tuple-element.2404, s32[]{:T(128)S(6)} %min.21, bf16[1,1,256,2048]{3,2,1,0:T(8,128)(2,1)} %constant_dynamic-slice_fusion.24, pred[]{:T(512)S(6)} %and.21, ...), kind=kOutput, calls=%fused_computation.47.clone.1 | convolution fusion | flops 1110441984 | bytes 9979909 | tf_op jit(solution)/shard_map/while/body/eval_jaxpr/bsd,df->bsf/dot_general | solution.py:99
  273.0 38.4 %all-reduce.11.cloned.1.call-done = f32[1,256,1024]{2,1,0:T(8,128)} async-done(((f32[1,256,1024]{2,1,0:T(8,128)}), f32[1,256,1024]{2,1,0:T(8,128)}) %all-reduce.11.cloned.1.call-update) | async-done | bytes 1048592 | tf_op jit(solution)/shard_map/while/body/eval_jaxpr/psum | solution.py:263
  321.8 8.1 %collective-permute-done = bf16[1,256,1024]{2,1,0:T(8,128)(2,1)} collective-permute-done((bf16[1,256,1024]{2,1,0:T(8,128)(2,1)S(1)}, bf16[1,256,1024]{2,1,0:T(8,128)(2,1)}, u32[]{:S(2)}, u32[]{:S(2)}) %collective-permute-start) | collective-permute-done | bytes 524320 | tf_op jit(solution)/shard_map/while/body/eval_jaxpr/ppermute | solution.py:16
  331.1 266.6 %while.79 = (s32[]{:T(128)}, bf16[1,256,1024]{2,1,0:T(8,128)(2,1)S(1)}, f32[1024]{0:T(1024)}, f32[1024]{0:T(1024)}, f32[1024]{0:T(1024)}, /*index=5*/f32[1024]{0...) while((s32[]{:T(128)}, ...), condition=%wide.region_20.21_spmd.clone, body=%wide.region_7.20_spmd.clone.sunk | while | flops 6822872064 | bytes 187449776 | solution.py:347
  373.8 27.8 %all-reduce.13.cloned.1.call-done = (bf16[1,256,1024]{2,1,0:T(8,128)(2,1)}, bf16[1,256,1024]{2,1,0:T(8,128)(2,1)}) async-done(((bf16[1,256,1024]{2,1,0:T(8,128)(2,1)}, bf16[1,256,1024]{2,1,0:T(8,128)(2,1)}), (bf16[1,256,1024]{2,1,0:T(8,128)(2,1)}, bf16[1,256,1024]{2,1,0:T(8,128)(2,1)})) %all-reduce.13.cloned.1.call-update) | async-done | bytes 1048592 | tf_op jit(solution)/shard_map/while/body/eval_jaxpr/psum | solution.py:307
  407.4 14.7 %collective-permute-done.1 = bf16[1,256,1024]{2,1,0:T(8,128)(2,1)S(1)} collective-permute-done((bf16[1,256,1024]{2,1,0:T(8,128)(2,1)S(1)}, bf16[1,256,1024]{2,1,0:T(8,128)(2,1)S(1)}, u32[]{:S(2)}, u32[]{:S(2)}) %collective-permute-start.1) | collective-permute-done | bytes 524320 | tf_op jit(solution)/shard_map/while/body/eval_jaxpr/ppermute | solution.py:16
  447.2 7.0 select_add_fusion.22
  454.2 8.2 %select_add_fusion.28 = f32[2048,1024]{1,0:T(8,128)} fusion(f32[2048,1024]{1,0:T(8,128)} %get-tuple-element.2512, pred[]{:T(512)S(6)} %compare.3, pred[]{:T(512)S(6)} %and.22, bf16[2,1,256,2048]{3,2,1,0:T(8,128)(2,1)S(1)} %copy-done.2, s32[]{:T(128)S(6)} %min.22, bf16[1,256,1024]{2,1,0:T(8,128)(2,1)S(1)} %get-tuple-element.2328), kind=kOutput, calls=%fused_computation.108.clone.1 | convolution fusion | flops 1080033280 | bytes 18350086 | tf_op jit(solution)/shard_map/while/body/eval_jaxpr/bsf,bsd->fd/dot_general | solution.py:155
  467.3 8.1 %select_add_fusion.26 = f32[1024,2048]{1,0:T(8,128)} fusion(f32[1024,2048]{1,0:T(8,128)} %get-tuple-element.2510, bf16[256,2048]{1,0:T(8,128)(2,1)S(1)} %copy-done.10, pred[]{:T(512)S(6)} %compare.3, pred[]{:T(512)S(6)} %and.22, bf16[2,1,256,1024]{3,2,1,0:T(8,128)(2,1)S(1)} %copy-done.8, s32[]{:T(128)S(6)} %min.22), kind=kOutput, calls=%fused_computation.109.clone.1 | convolution fusion | flops 1080033280 | bytes 18350086 | tf_op jit(solution)/shard_map/while/body/eval_jaxpr/bsd,bsf->df/dot_general | solution.py:161
  475.4 13.8 %all-reduce.13.cloned.1.call-done = (bf16[1,256,1024]{2,1,0:T(8,128)(2,1)}, bf16[1,256,1024]{2,1,0:T(8,128)(2,1)}) async-done(((bf16[1,256,1024]{2,1,0:T(8,128)(2,1)}, bf16[1,256,1024]{2,1,0:T(8,128)(2,1)}), (bf16[1,256,1024]{2,1,0:T(8,128)(2,1)}, bf16[1,256,1024]{2,1,0:T(8,128)(2,1)})) %all-reduce.13.cloned.1.call-update) | async-done | bytes 1048592 | tf_op jit(solution)/shard_map/while/body/eval_jaxpr/psum | solution.py:307
  495.0 14.7 %collective-permute-done.1 = bf16[1,256,1024]{2,1,0:T(8,128)(2,1)S(1)} collective-permute-done((bf16[1,256,1024]{2,1,0:T(8,128)(2,1)S(1)}, bf16[1,256,1024]{2,1,0:T(8,128)(2,1)S(1)}, u32[]{:S(2)}, u32[]{:S(2)}) %collective-permute-start.1) | collective-permute-done | bytes 524320 | tf_op jit(solution)/shard_map/while/body/eval_jaxpr/ppermute | solution.py:16
  534.8 7.0 select_add_fusion.22
  541.9 8.2 %select_add_fusion.28 = f32[2048,1024]{1,0:T(8,128)} fusion(f32[2048,1024]{1,0:T(8,128)} %get-tuple-element.2512, pred[]{:T(512)S(6)} %compare.3, pred[]{:T(512)S(6)} %and.22, bf16[2,1,256,2048]{3,2,1,0:T(8,128)(2,1)S(1)} %copy-done.2, s32[]{:T(128)S(6)} %min.22, bf16[1,256,1024]{2,1,0:T(8,128)(2,1)S(1)} %get-tuple-element.2328), kind=kOutput, calls=%fused_computation.108.clone.1 | convolution fusion | flops 1080033280 | bytes 18350086 | tf_op jit(solution)/shard_map/while/body/eval_jaxpr/bsf,bsd->fd/dot_general | solution.py:155
  555.0 8.1 %select_add_fusion.26 = f32[1024,2048]{1,0:T(8,128)} fusion(f32[1024,2048]{1,0:T(8,128)} %get-tuple-element.2510, bf16[256,2048]{1,0:T(8,128)(2,1)S(1)} %copy-done.10, pred[]{:T(512)S(6)} %compare.3, pred[]{:T(512)S(6)} %and.22, bf16[2,1,256,1024]{3,2,1,0:T(8,128)(2,1)S(1)} %copy-done.8, s32[]{:T(128)S(6)} %min.22), kind=kOutput, calls=%fused_computation.109.clone.1 | convolution fusion | flops 1080033280 | bytes 18350086 | tf_op jit(solution)/shard_map/while/body/eval_jaxpr/bsd,bsf->df/dot_general | solution.py:161
  563.1 13.8 %all-reduce.13.cloned.1.call-done = (bf16[1,256,1024]{2,1,0:T(8,128)(2,1)}, bf16[1,256,1024]{2,1,0:T(8,128)(2,1)}) async-done(((bf16[1,256,1024]{2,1,0:T(8,128)(2,1)}, bf16[1,256,1024]{2,1,0:T(8,128)(2,1)}), (bf16[1,256,1024]{2,1,0:T(8,128)(2,1)}, bf16[1,256,1024]{2,1,0:T(8,128)(2,1)})) %all-reduce.13.cloned.1.call-update) | async-done | bytes 1048592 | tf_op jit(solution)/shard_map/while/body/eval_jaxpr/psum | solution.py:307
  582.7 14.7 %collective-permute-done.1 = bf16[1,256,1024]{2,1,0:T(8,128)(2,1)S(1)} collective-permute-done((bf16[1,256,1024]{2,1,0:T(8,128)(2,1)S(1)}, bf16[1,256,1024]{2,1,0:T(8,128)(2,1)S(1)}, u32[]{:S(2)}, u32[]{:S(2)}) %collective-permute-start.1) | collective-permute-done | bytes 524320 | tf_op jit(solution)/shard_map/while/body/eval_jaxpr/ppermute | solution.py:16
  615.7 125.2 %all-reduce.1 = (bf16[1,1024]{1,0:T(2,128)(2,1)S(1)}, bf16[1,1024]{1,0:T(2,128)(2,1)S(1)}, bf16[1,1024]{1,0:T(2,128)(2,1)S(1)}, bf16[1,1024]{1,0:T(2,128)(2,1)S(...) all-reduce(bf16[1,1024]{1,0:T(2,128)(2,1)S(1)} %broadcast_in_dim.38, ...), channel_id=1, replica_groups=mesh['section'=2,'dp'=32,'tensor'=2] {'dp'}, use_global_device_ids=true, to_apply=%region_21.22 | all-reduce | flops 8704 | bytes 34816 | tf_op jit(solution)/shard_map/psum | solution.py:351
  (772 shorter events, 302.8 us)
Async XLA Ops:
  28.7 81.9 %all-reduce.11.cloned.1.call-start = ((), (), s32[]{:S(2)}) async-start(), calls=%async_computation.1 | async-start | bytes 2097152 | tf_op jit(solution)/shard_map/while/body/eval_jaxpr/psum | solution.py:263
  70.9 39.7 %copy-start.35 = (f32[1024]{0:T(1024)S(1)}, f32[1024]{0:T(1024)}, u32[]{:S(2)}) copy-start(f32[1024]{0:T(1024)} %copy-done.34) | copy-start | bytes 12292 | tf_op jit(solution)/shard_map/while
  114.1 14.9 %collective-permute-start = (bf16[1,256,1024]{2,1,0:T(8,128)(2,1)S(1)}, bf16[1,256,1024]{2,1,0:T(8,128)(2,1)}, u32[]{:S(2)}, u32[]{:S(2)}) collective-permute-start(bf16[1,256,1024]{2,1,0:T(8,128)(2,1)S(1)} %get-tuple-element.2280), channel_id=1, source_target_pairs={{0,64},{1,65},{2,66},{3,67},{4,68},{5,69},{6,70},{7,71},{8,72},{9,... | collective-permute-start | bytes 1572872 | tf_op jit(solution)/shard_map/while/body/eval_jaxpr/ppermute | solution.py:16
  129.1 81.9 %all-reduce.11.cloned.1.call-start = ((), (), s32[]{:S(2)}) async-start(), calls=%async_computation.1 | async-start | bytes 2097152 | tf_op jit(solution)/shard_map/while/body/eval_jaxpr/psum | solution.py:263
  171.3 39.8 %copy-start.35 = (f32[1024]{0:T(1024)S(1)}, f32[1024]{0:T(1024)}, u32[]{:S(2)}) copy-start(f32[1024]{0:T(1024)} %copy-done.34) | copy-start | bytes 12292 | tf_op jit(solution)/shard_map/while
  171.3 39.8 %copy-start.37 = (f32[1024]{0:T(1024)S(1)}, f32[1024]{0:T(1024)}, u32[]{:S(2)}) copy-start(f32[1024]{0:T(1024)} %copy-done.36) | copy-start | bytes 12292 | tf_op jit(solution)/shard_map/while
  171.3 39.8 %copy-start.38 = (f32[1024]{0:T(1024)S(1)}, f32[1024]{0:T(1024)}, u32[]{:S(2)}) copy-start(f32[1024]{0:T(1024)} %convert_element_type.646) | copy-start | bytes 12292 | tf_op jit(solution)/shard_map/while
  171.3 39.8 %copy-start.39 = (f32[1024]{0:T(1024)S(1)}, f32[1024]{0:T(1024)}, u32[]{:S(2)}) copy-start(f32[1024]{0:T(1024)} %convert_element_type.647) | copy-start | bytes 12292 | tf_op jit(solution)/shard_map/while
  171.3 39.8 %copy-start.48 = (f32[1024]{0:T(1024)S(1)}, f32[1024]{0:T(1024)}, u32[]{:S(2)}) copy-start(f32[1024]{0:T(1024)} %get-tuple-element.2456) | copy-start | bytes 12292 | tf_op jit(solution)/shard_map/while
  214.6 14.9 %collective-permute-start = (bf16[1,256,1024]{2,1,0:T(8,128)(2,1)S(1)}, bf16[1,256,1024]{2,1,0:T(8,128)(2,1)}, u32[]{:S(2)}, u32[]{:S(2)}) collective-permute-start(bf16[1,256,1024]{2,1,0:T(8,128)(2,1)S(1)} %get-tuple-element.2280), channel_id=1, source_target_pairs={{0,64},{1,65},{2,66},{3,67},{4,68},{5,69},{6,70},{7,71},{8,72},{9,... | collective-permute-start | bytes 1572872 | tf_op jit(solution)/shard_map/while/body/eval_jaxpr/ppermute | solution.py:16
  229.5 81.9 %all-reduce.11.cloned.1.call-start = ((), (), s32[]{:S(2)}) async-start(), calls=%async_computation.1 | async-start | bytes 2097152 | tf_op jit(solution)/shard_map/while/body/eval_jaxpr/psum | solution.py:263
  271.7 39.8 %copy-start.35 = (f32[1024]{0:T(1024)S(1)}, f32[1024]{0:T(1024)}, u32[]{:S(2)}) copy-start(f32[1024]{0:T(1024)} %copy-done.34) | copy-start | bytes 12292 | tf_op jit(solution)/shard_map/while
  271.7 39.8 %copy-start.37 = (f32[1024]{0:T(1024)S(1)}, f32[1024]{0:T(1024)}, u32[]{:S(2)}) copy-start(f32[1024]{0:T(1024)} %copy-done.36) | copy-start | bytes 12292 | tf_op jit(solution)/shard_map/while
  271.7 39.8 %copy-start.38 = (f32[1024]{0:T(1024)S(1)}, f32[1024]{0:T(1024)}, u32[]{:S(2)}) copy-start(f32[1024]{0:T(1024)} %convert_element_type.646) | copy-start | bytes 12292 | tf_op jit(solution)/shard_map/while
  271.7 39.7 %copy-start.39 = (f32[1024]{0:T(1024)S(1)}, f32[1024]{0:T(1024)}, u32[]{:S(2)}) copy-start(f32[1024]{0:T(1024)} %convert_element_type.647) | copy-start | bytes 12292 | tf_op jit(solution)/shard_map/while
  271.7 39.7 %copy-start.48 = (f32[1024]{0:T(1024)S(1)}, f32[1024]{0:T(1024)}, u32[]{:S(2)}) copy-start(f32[1024]{0:T(1024)} %get-tuple-element.2456) | copy-start | bytes 12292 | tf_op jit(solution)/shard_map/while
  315.0 14.9 %collective-permute-start = (bf16[1,256,1024]{2,1,0:T(8,128)(2,1)S(1)}, bf16[1,256,1024]{2,1,0:T(8,128)(2,1)}, u32[]{:S(2)}, u32[]{:S(2)}) collective-permute-start(bf16[1,256,1024]{2,1,0:T(8,128)(2,1)S(1)} %get-tuple-element.2280), channel_id=1, source_target_pairs={{0,64},{1,65},{2,66},{3,67},{4,68},{5,69},{6,70},{7,71},{8,72},{9,... | collective-permute-start | bytes 1572872 | tf_op jit(solution)/shard_map/while/body/eval_jaxpr/ppermute | solution.py:16
  331.1 70.5 %all-reduce.13.cloned.1.call-start = ((), (), s32[]{:S(2)}) async-start(), calls=%async_computation.2 | async-start | bytes 2097152 | tf_op jit(solution)/shard_map/while/body/eval_jaxpr/psum | solution.py:307
  405.9 16.2 %collective-permute-start.1 = (bf16[1,256,1024]{2,1,0:T(8,128)(2,1)S(1)}, bf16[1,256,1024]{2,1,0:T(8,128)(2,1)S(1)}, u32[]{:S(2)}, u32[]{:S(2)}) collective-permute-start(bf16[1,256,1024]{2,1,0:T(8,128)(2,1)S(1)} %get-tuple-element.2346), channel_id=1, source_target_pairs={{64,0},{65,1},{66,2},{67,3},{68,4},{69,5},{70,6},{71,7},{72,8},{73... | collective-permute-start | bytes 1572872 | tf_op jit(solution)/shard_map/while/body/eval_jaxpr/ppermute | solution.py:16
  422.2 67.1 %all-reduce.13.cloned.1.call-start = ((), (), s32[]{:S(2)}) async-start(), calls=%async_computation.2 | async-start | bytes 2097152 | tf_op jit(solution)/shard_map/while/body/eval_jaxpr/psum | solution.py:307
  493.6 16.2 %collective-permute-start.1 = (bf16[1,256,1024]{2,1,0:T(8,128)(2,1)S(1)}, bf16[1,256,1024]{2,1,0:T(8,128)(2,1)S(1)}, u32[]{:S(2)}, u32[]{:S(2)}) collective-permute-start(bf16[1,256,1024]{2,1,0:T(8,128)(2,1)S(1)} %get-tuple-element.2346), channel_id=1, source_target_pairs={{64,0},{65,1},{66,2},{67,3},{68,4},{69,5},{70,6},{71,7},{72,8},{73... | collective-permute-start | bytes 1572872 | tf_op jit(solution)/shard_map/while/body/eval_jaxpr/ppermute | solution.py:16
  509.8 67.1 %all-reduce.13.cloned.1.call-start = ((), (), s32[]{:S(2)}) async-start(), calls=%async_computation.2 | async-start | bytes 2097152 | tf_op jit(solution)/shard_map/while/body/eval_jaxpr/psum | solution.py:307
  581.2 16.2 %collective-permute-start.1 = (bf16[1,256,1024]{2,1,0:T(8,128)(2,1)S(1)}, bf16[1,256,1024]{2,1,0:T(8,128)(2,1)S(1)}, u32[]{:S(2)}, u32[]{:S(2)}) collective-permute-start(bf16[1,256,1024]{2,1,0:T(8,128)(2,1)S(1)} %get-tuple-element.2346), channel_id=1, source_target_pairs={{64,0},{65,1},{66,2},{67,3},{68,4},{69,5},{70,6},{71,7},{72,8},{73... | collective-permute-start | bytes 1572872 | tf_op jit(solution)/shard_map/while/body/eval_jaxpr/ppermute | solution.py:16
  597.7 151.2 %all-reduce.9.cloned.1.call-start = ((), (), s32[]{:S(2)}) async-start(), calls=%async_computation | async-start | bytes 25165824 | tf_op jit(solution)/shard_map/psum | solution.py:355
  (204 other events, 1353.4 us)
Sparse Core Ops, SparseCore 0:
  60.6 49.9 all-reduce.10
  161.0 50.0 all-reduce.10
  261.4 50.0 all-reduce.10
  351.5 50.0 all-reduce.12
  442.7 46.5 all-reduce.12
  530.3 46.5 all-reduce.12
Sparse Core Ops, SparseCore 1:
  615.0 133.9 all-reduce.8
where the time goes:
time: 776 us; the launch traced here: 772 us
  waiting for transfers between devices  244 us (31%)
  matrix products  167 us (22%)
  blocking collectives  125 us (16%)
  other arithmetic  109 us (14%)
  local copies, waits for them, and re-layouts  77.3 us (10%)
  starting transfers between devices  19.5 us (3%)
  between operations  15.8 us (2%)
  loops' own time  15.2 us (2%)
    psum x1, blocking collectives, shards(): lax.psum(totals[0].astype(jnp.bfloat16), 'dp').astype(jnp.float32)  125 us
    psum x3, waiting for transfers between devices, forward_tick(): summed = lax.psum(branch_sum, 'tensor')  115 us
    ppermute x6, waiting for transfers between devices, passed_along(): lax.ppermute(value, axis, [(source, source + steps) for source in range(l...  68.5 us
    psum x3, waiting for transfers between devices, backward_tick(): lax.psum(d_second.astype(jnp.bfloat16), 'tensor').astype(jnp.float32)  55.4 us
    dynamic_update_slice x24, other arithmetic, put_slot(): lax.dynamic_update_index_in_dim(stored, jnp.where(is_valid, value, previo...  31.5 us
    dot_general x3, matrix products, forward_local(): jnp.einsum('bsd,df->bsf', second_in, up_w, preferred_element_type=jnp.flo...  27.6 us
    dynamic_slice x18, local copies, waits for them, and re-layouts, put_slot(): previous = lax.dynamic_index_in_dim(stored, index, 0, keepdims=False)  24.4 us
    dot_general x3, matrix products, backward_local(): jnp.einsum('bsf,bsd->fd', activated, upstream, preferred_element_type=jnp...  21.1 us
  transfers between devices with their start and end apart: 13, of which 13 were waited for; matrix products, arithmetic and copies ran while one was open for 15% of the time, Pallas kernels for 0%

commit v1 on v0

--- a/solution.py
+++ b/solution.py
@@ -1,7 +1,340 @@
+import functools
 import jax
 import jax.numpy as jnp
 from jax import lax
+from jax.experimental import pallas as pl
+from jax.experimental.pallas import tpu as pltpu
 from jax.sharding import PartitionSpec as P
+
+MESH = pl.DeviceIdType.MESH
+
+SLABS = 6
+SLAB_ROWS = 2048
+HALF = 1024
+STREAM = 512
+COLS = 512
+CHUNK = (128, 32)
+RX_ONE = (0, 768)
+RX_TWO = (256, 832)
+RX_ROWS = 960
+SMALL = 32
+
+
+def mod4(value):
+    return lax.rem(value + 4, 4)
+
+
+class Place:
+    def __init__(self):
+        self.section = lax.axis_index("section")
+        self.tensor = lax.axis_index("tensor")
+        dp = lax.axis_index("dp")
+        self.core = lax.rem(dp, 2)
+        self.x = lax.rem(dp // 2, 4)
+        self.z = dp // 8
+
+    def at(self, z, x, core):
+        return (self.section, (z * 4 + x) * 2 + core, self.tensor)
+
+    def other_core(self):
+        return self.at(self.z, self.x, 1 - self.core)
+
+    def along(self, axis, step):
+        if axis == 0:
+            return self.at(self.z, mod4(self.x + step), self.core)
+        return self.at(mod4(self.z + step), self.x, self.core)
+
+    def position(self, axis):
+        return self.x if axis == 0 else self.z
+
+
+def ds(start, size):
+    return pl.ds(pl.multiple_of(start, 16), size)
+
+
+def take(ref, sem):
+    pltpu.make_async_copy(ref, ref, sem).wait()
+
+
+def put(src, dst, send_sem, recv_sem, device):
+    pltpu.make_async_remote_copy(
+        src_ref=src, dst_ref=dst, send_sem=send_sem, recv_sem=recv_sem,
+        device_id=device, device_id_type=MESH,
+    ).start()
+
+
+def added(*parts):
+    total = parts[0].astype(jnp.float32)
+    for part in parts[1:]:
+        total = total + part.astype(jnp.float32)
+    return total.astype(jnp.bfloat16)
+
+
+class Reduce:
+    def __init__(self, place, grads, out, arrived, landing, send, recv):
+        self.place, self.grads, self.out = place, grads, out
+        self.arrived, self.landing, self.send, self.recv = arrived, landing, send, recv
+
+    def base(self, stream):
+        return self.place.core * HALF + stream * STREAM
+
+    def layout(self, stream, phase):
+        axis = (stream + phase) % 2
+        p = self.place.position(axis)
+        start = self.base(stream)
+        if phase == 1:
+            start = start + self.place.position(stream) * CHUNK[0]
+        return axis, p, start, CHUNK[phase]
+
+    def first_sends(self, s, phase, sem):
+        h = CHUNK[phase] // 2
+        for stream in range(2):
+            axis, p, start, size = self.layout(stream, phase)
+            far = start + mod4(p + 2) * size
+            for side, step in ((0, 1), (1, -1)):
+                put(self.grads.at[s, ds(far + side * h, h)],
+                    self.landing.at[s, pl.ds(RX_ONE[phase] + (stream * 2 + side) * h, h)],
+                    self.send.at[s, 0], self.recv.at[s, sem], self.place.along(axis, step))
+
+    def second_sends(self, s, phase, sem):
+        h = CHUNK[phase] // 2
+        take(self.landing.at[s, pl.ds(0, 4 * h)], self.recv.at[s, sem - 1])
+        for stream in range(2):
+            axis, p, start, size = self.layout(stream, phase)
+            for side, step in ((0, 1), (1, -1)):
+                near = start + mod4(p + step) * size
+                rows = ds(near + side * h, h)
+                came = pl.ds(RX_ONE[phase] + (stream * 2 + side) * h, h)
+                self.grads[s, rows] = added(self.grads[s, rows], self.landing[s, came])
+                put(self.grads.at[s, ds(near, size)],
+                    self.landing.at[s, pl.ds(RX_TWO[phase] + (stream * 2 + side) * size, size)],
+                    self.send.at[s, 0], self.recv.at[s, sem], self.place.along(axis, step))
+
+    def finish(self, s, phase, sem, target):
+        size = CHUNK[phase]
+        take(self.landing.at[s, pl.ds(0, 4 * size)], self.recv.at[s, sem])
+        for stream in range(2):
+            axis, p, start, size = self.layout(stream, phase)
+            rows = ds(start + p * size, size)
+            left = pl.ds(RX_TWO[phase] + stream * 2 * size, size)
+            right = pl.ds(RX_TWO[phase] + (stream * 2 + 1) * size, size)
+            target[s, rows] = added(self.grads[s, rows], self.landing[s, left], self.landing[s, right])
+
+    def spread(self, s, phase, sem):
+        for stream in range(2):
+            axis, p, start, size = self.layout(stream, phase)
+            rows = ds(start + p * size, size)
+            for step in (1, -1):
+                put(self.out.at[s, rows], self.out.at[s, rows], self.send.at[s, 1],
+                    self.recv.at[s, sem], self.place.along(axis, step))
+
+    def forward(self, s, phase, sem):
+        size = CHUNK[phase]
+        take(self.out.at[s, pl.ds(0, 4 * size)], self.recv.at[s, sem - 1])
+        for stream in range(2):
+            axis, p, start, size = self.layout(stream, phase)
+            for side, step in ((0, 1), (1, -1)):
+                rows = ds(start + mod4(p - step) * size + side * (size // 2), size // 2)
+                put(self.out.at[s, rows], self.out.at[s, rows], self.send.at[s, 1],
+                    self.recv.at[s, sem], self.place.along(axis, step))
+
+    def to_core(self, s, offsets):
+        for stream in range(2):
+            axis, p, start, size = self.layout(stream, 0)
+            for offset in offsets:
+                rows = ds(start + mod4(p + offset) * size, size)
+                put(self.out.at[s, rows], self.out.at[s, rows], self.send.at[s, 1],
+                    self.recv.at[s, 9], self.place.other_core())
+
+    def step(self, s, k):
+        core = self.place.core
+        if k == 0:
+            put(self.grads.at[s, ds((1 - core) * HALF, HALF)], self.arrived.at[s],
+                self.send.at[s, 0], self.recv.at[s, 0], self.place.other_core())
+        elif k == 1:
+            take(self.arrived.at[s], self.recv.at[s, 0])
+
+            def block(i, _):
+                here = ds(core * HALF + i * 128, 128)
+                self.grads[s, here] = added(self.grads[s, here], self.arrived[s, ds(i * 128, 128)])
+                return 0
+
+            lax.fori_loop(0, HALF // 128, block, 0)
+            self.first_sends(s, 0, 1)
+        elif k == 2:
+            self.second_sends(s, 0, 2)
+        elif k == 3:
+            self.finish(s, 0, 2, self.grads)
+            self.first_sends(s, 1, 3)
+        elif k == 4:
+            self.second_sends(s, 1, 4)
+        elif k == 5:
+            self.finish(s, 1, 4, self.out)
+            self.spread(s, 1, 5)
+        elif k == 6:
+            self.forward(s, 1, 6)
+        elif k == 7:
+            take(self.out.at[s, pl.ds(0, 64)], self.recv.at[s, 6])
+            self.spread(s, 0, 7)
+            self.to_core(s, (0,))
+        elif k == 8:
+            self.forward(s, 0, 8)
+            self.to_core(s, (1, -1))
+        elif k == 9:
+            take(self.out.at[s, pl.ds(0, 256)], self.recv.at[s, 8])
+            self.to_core(s, (2,))
+        elif k == 10:
+            take(self.out.at[s, pl.ds(0, 1024)], self.recv.at[s, 9])
+
+    def drain(self, s):
+        take(self.grads.at[s, pl.ds(0, 1984)], self.send.at[s, 0])
+        take(self.grads.at[s, pl.ds(0, 1984)], self.send.at[s, 1])
+
+
+class SmallReduce:
+    def __init__(self, place, mine, out, landing, pair, send, recv):
+        self.place, self.mine, self.out, self.landing, self.pair = place, mine, out, landing, pair
+        self.send, self.recv = send, recv
+
+    def exchange(self, axis):
+        p = self.place.position(axis)
+        for step in (1, 2, 3):
+            put(self.landing.at[axis, p], self.landing.at[axis, p], self.send, self.recv.at[1 + axis],
+                self.place.along(axis, step))
+
+    def collected(self, axis):
+        take(self.landing.at[axis, pl.ds(0, 3)], self.recv.at[1 + axis])
+        return added(*[self.landing[axis, j] for j in range(4)])
+
+    def step(self, k):
+        half = SMALL // 2
+        rows = ds(self.place.core * half, half)
+        if k == 0:
+            put(self.mine, self.pair, self.send, self.recv.at[0], self.place.other_core())
+        elif k == 1:
+            take(self.pair, self.recv.at[0])
+            self.landing[0, self.place.x] = added(self.mine[rows], self.pair[rows])
+            self.exchange(0)
+        elif k == 2:
+            self.landing[1, self.place.z] = self.collected(0)
+            self.exchange(1)
+        elif k == 3:
+            self.out[rows] = self.collected(1)
+            put(self.out.at[rows], self.out.at[rows], self.send, self.recv.at[3], self.place.other_core())
+        elif k == 4:
+            take(self.out.at[pl.ds(0, half)], self.recv.at[3])
+
+    def drain(self):
+        half = SMALL // 2
+        take(self.landing.at[0, pl.ds(0, 3)], self.send)
+        take(self.landing.at[0, pl.ds(0, 3)], self.send)
+        take(self.mine, self.send)
+        take(self.out.at[pl.ds(0, half)], self.send)
+
+
+def greet(devices):
+    barrier = pltpu.get_barrier_semaphore()
+    for device in devices:
+        pl.semaphore_signal(barrier, inc=1, device_id=device, device_id_type=MESH)
+    pl.semaphore_wait(barrier, len(devices))
+
+
+def plane_partners(place):
+    return [place.other_core()] + [place.along(axis, step) for axis in (0, 1) for step in (1, 2, 3)]
+
+ORDER = (
+    (0, 0), (1, 0), (2, 0), (3, 0), (4, 0), (5, 0), (0, 1), (1, 1),
+    (2, 1), (0, 2), (3, 1), (1, 2), (4, 1), (2, 2), (5, 1), (0, 3),
+    (3, 2), (1, 3), (4, 2), (2, 3), (5, 2), (0, 4), (3, 3), (1, 4),
+    (4, 3), (2, 4), (5, 3), (0, 5), (3, 4), (1, 5), (4, 4), (2, 5),
+    (5, 4), (0, 6), (3, 5), (1, 6), (4, 5), (2, 6), (5, 5), (0, 7),
+    (3, 6), (1, 7), (4, 6), (2, 7), (5, 6), (0, 8), (3, 7), (1, 8),
+    (4, 7), (2, 8), (5, 7), (0, 9), (3, 8), (1, 9), (4, 8), (2, 9),
+    (5, 8), (3, 9), (4, 9), (5, 9),
+)
+
+
+def reduce_kernel(given, small_in, out, small_out, grads, arrived, landing, mine, small_landing, pair,
+                  send, recv, small_send, small_recv, load):
+    place = Place()
+    for s in range(SLABS):
+        pltpu.make_async_copy(given.at[s], grads.at[s], load.at[s]).start()
+    greet(plane_partners(place))
+    mine[...] = small_in[...]
+    reduce = Reduce(place, grads, out, arrived, landing, send, recv)
+    small = SmallReduce(place, mine, small_out, small_landing, pair, small_send, small_recv)
+    small.step(0)
+    small_step = 1
+    for turn, (s, k) in enumerate(ORDER):
+        if k == 0:
+            pltpu.make_async_copy(given.at[s], grads.at[s], load.at[s]).wait()
+        reduce.step(s, k)
+        if turn in (12, 20, 28, 36):
+            small.step(small_step)
+            small_step += 1
+    for s in range(SLABS):
+        reduce.step(s, 10)
+    for s in range(SLABS):
+        reduce.drain(s)
+    small.drain()
+
+
+def all_reduce(grads, small):
+    bf16, dma = jnp.bfloat16, pltpu.SemaphoreType.DMA
+    half = SMALL // 2
+    return pl.pallas_call(
+        reduce_kernel,
+        out_shape=(pltpu.VMEM((SLABS, SLAB_ROWS, COLS), bf16), pltpu.VMEM((SMALL, COLS), bf16)),
+        in_specs=[pl.BlockSpec(memory_space=pl.ANY), pl.BlockSpec(memory_space=pltpu.VMEM)],
+        out_specs=(pl.BlockSpec(memory_space=pltpu.VMEM), pl.BlockSpec(memory_space=pltpu.VMEM)),
+        scratch_shapes=[
+            pltpu.VMEM((SLABS, SLAB_ROWS, COLS), bf16),
+            pltpu.VMEM((SLABS, HALF, COLS), bf16),
+            pltpu.VMEM((SLABS, RX_ROWS, COLS), bf16),
+            pltpu.VMEM((SMALL, COLS), bf16),
+            pltpu.VMEM((2, 4, half, COLS), bf16),
+            pltpu.VMEM((SMALL, COLS), bf16),
+            dma((SLABS, 2)),
+            dma((SLABS, 10)),
+            dma,
+            dma((4,)),
+            dma((SLABS,)),
+        ],
+        compiler_params=pltpu.CompilerParams(
+            collective_id=0, has_side_effects=True, vmem_limit_bytes=28 * 2**20
+        ),
+    )(grads, small)
+
+
+def halves(matrix):
+    return jnp.stack([matrix[:, :COLS], matrix[:, COLS:]])
+
+
+def packed(totals):
+    totals = [t.astype(jnp.bfloat16) for t in totals]
+    qkv, out, up, down = totals[4], totals[6], totals[8], totals[10]
+    up_slabs = up.reshape(1024, 4, COLS).transpose(1, 0, 2).reshape(2, SLAB_ROWS, COLS)
+    qkv_part = qkv.transpose(1, 0, 2).reshape(3 * 1024, COLS)
+    last = jnp.concatenate([halves(out).reshape(1024, COLS), qkv_part]).reshape(2, SLAB_ROWS, COLS)
+    grads = jnp.concatenate([halves(down), up_slabs, last])
+    small = jnp.concatenate([totals[i].reshape(-1) for i in (0, 1, 2, 3, 5, 7, 9)])
+    small = jnp.pad(small, (0, SMALL * COLS - small.shape[0])).reshape(SMALL, COLS)
+    return grads, small
+
+
+def unpacked(grads, small):
+    small = small.reshape(-1).astype(jnp.float32)
+    down = jnp.concatenate([grads[0], grads[1]], axis=1)
+    up = grads[2:4].reshape(4, 1024, COLS).transpose(1, 0, 2).reshape(1024, 4 * COLS)
+    last = grads[4:6].reshape(4, 1024, COLS)
+    out = last[0].reshape(2, COLS, COLS).transpose(1, 0, 2).reshape(COLS, 2 * COLS)
+    qkv = last[1:].transpose(1, 0, 2)
+    return (
+        small[0:1024], small[1024:2048], small[2048:3072], small[3072:4096],
+        qkv.astype(jnp.float32), small[4096:5632].reshape(3, COLS), out.astype(jnp.float32),
+        small[5632:6656], up.astype(jnp.float32), small[6656:8704], down.astype(jnp.float32),
+    )
+
 
 HD = 64
 ROT = 16
@@ -347,19 +680,7 @@
     arriving, totals, grad_store = lax.fori_loop(
         0, tick_count, backward_tick, (empty_rows, zero_grads, grad_store)
     )
-    totals = (
-        lax.psum(totals[0].astype(jnp.bfloat16), "dp").astype(jnp.float32),
-        lax.psum(totals[1].astype(jnp.bfloat16), "dp").astype(jnp.float32),
-        lax.psum(totals[2].astype(jnp.bfloat16), "dp").astype(jnp.float32),
-        lax.psum(totals[3].astype(jnp.bfloat16), "dp").astype(jnp.float32),
-        lax.psum(totals[4].astype(jnp.bfloat16), "dp").astype(jnp.float32),
-        lax.psum(totals[5].astype(jnp.bfloat16), "dp").astype(jnp.float32),
-        lax.psum(totals[6].astype(jnp.bfloat16), "dp").astype(jnp.float32),
-        lax.psum(totals[7].astype(jnp.bfloat16), "dp").astype(jnp.float32),
-        lax.psum(totals[8].astype(jnp.bfloat16), "dp").astype(jnp.float32),
-        lax.psum(totals[9].astype(jnp.bfloat16), "dp").astype(jnp.float32),
-        lax.psum(totals[10].astype(jnp.bfloat16), "dp").astype(jnp.float32),
-    )
+    totals = unpacked(*all_reduce(*packed(totals)))
     return (
         out_store[None],
         grad_store[None],

time: 776 us -> 758 us (0.977)
  blocking collectives: 125 us -> 0 us
  Pallas kernels: 0 us -> 77.5 us
  local copies, waits for them, and re-layouts: 77.3 us -> 110 us
    psum x1 -> x0, blocking collectives: 125 us -> none  [shards(): lax.psum(totals[0].astype(jnp.bfloat16), 'dp').astype(jnp.float32)]
    pallas_call x0 -> x1, Pallas kernels: none -> 77.5 us  [all_reduce(): pl.pallas_call(reduce_kernel, out_shape=(pltpu.VMEM((SLABS, SLAB_ROWS, CO...]
    broadcast_in_dim x13 -> x0, other arithmetic: 30.4 us -> none  [the longest x2 10.6 us: shards(): totals[10][None]]
    convert_element_type x0 -> x4, local copies, waits for them, and re-layouts: none -> 27 us  [the longest x2 22.9 us: unpacked(): up.astype(jnp.float32)]
    convert_element_type x7 -> x10, other arithmetic: 0.03 us -> 21.2 us  [the longest x7 9.79 us: packed(): totals = [t.astype(jnp.bfloat16) for t in totals]]
    unnamed x29 -> x24, local copies, waits for them, and re-layouts: 1.27 us -> 12 us
    dynamic_slice x12, local copies, waits for them, and re-layouts: 8.75 us -> 0.24 us  [backward_tick(): lax.dynamic_index_in_dim(entry, clipped, 0, keepdims=False)]
  transfers between devices with their start and end apart: 13 -> 12, of which waited for: 13 -> 12; matrix products, arithmetic and copies ran while one was open for 15% -> 15% of each run, Pallas kernels for 0% -> 0%
where the time goes in v1:
time: 758 us; the launch traced here: 747 us
  waiting for transfers between devices  240 us (32%)
  matrix products  167 us (22%)
  local copies, waits for them, and re-layouts  110 us (15%)
  other arithmetic  104 us (14%)
  Pallas kernels  77.5 us (10%)
  starting transfers between devices  19.4 us (3%)
  loops' own time  15 us (2%)
  between operations  14.8 us (2%)
    psum x3, waiting for transfers between devices, forward_tick(): summed = lax.psum(branch_sum, 'tensor')  115 us
    pallas_call x1, Pallas kernels, all_reduce(): pl.pallas_call(reduce_kernel, out_shape=(pltpu.VMEM((SLABS, SLAB_ROWS, CO...  77.5 us
    ppermute x6, waiting for transfers between devices, passed_along(): lax.ppermute(value, axis, [(source, source + steps) for source in range(l...  68.9 us
    psum x3, waiting for transfers between devices, backward_tick(): lax.psum(d_second.astype(jnp.bfloat16), 'tensor').astype(jnp.float32)  55.4 us
    dynamic_update_slice x24, other arithmetic, put_slot(): lax.dynamic_update_index_in_dim(stored, jnp.where(is_valid, value, previo...  31.4 us
    dot_general x3, matrix products, forward_local(): jnp.einsum('bsd,df->bsf', second_in, up_w, preferred_element_type=jnp.flo...  27.5 us
    dynamic_slice x18, local copies, waits for them, and re-layouts, put_slot(): previous = lax.dynamic_index_in_dim(stored, index, 0, keepdims=False)  24.4 us
    convert_element_type x2, local copies, waits for them, and re-layouts, unpacked(): up.astype(jnp.float32)  22.9 us
  transfers between devices with their start and end apart: 12, of which 12 were waited for; matrix products, arithmetic and copies ran while one was open for 15% of the time, Pallas kernels for 0%

profile of v1, /device:TPU:1, one launch (start us, length us, event | category | flops | bytes accessed | tf_op | source)
XLA Modules:
  0.0 746.8 jit_solution(14925254043989790078)
XLA Ops:
  27.8 300.8 %while.78 = (s32[]{:T(128)}, bf16[1,256,1024]{2,1,0:T(8,128)(2,1)}, f32[2,1,256,1024]{3,2,1,0:T(8,128)}, f32[2,1,256,1]{2,3,1,0:T(1,128)}, bf16[2,1,256,1024]{3,...) while((s32[]{:T(128)}, bf16[1,256,1024]{2,1,0:T(8,128)(2,1)}, ...), condition=%wide.region_6.7_spmd, body=%wide.region_0.6_spmd.sunk | while | flops 3409584128 | bytes 141941424 | solution.py:620
  46.3 9.2 %bitcast_dynamic-update-slice_fusion.10 = (bf16[2,1,256,2048]{3,2,1,0:T(8,128)(2,1)}, bf16[256,2048]{1,0:T(8,128)(2,1)S(1)}, f32[256,2048]{1,0:T(8,128)}) fusion(bf16[2,1,256,2048]{3,2,1,0:T(8,128)(2,1)} %get-tuple-element.2438, s32[]{:T(128)S(6)} %min.21, bf16[1,1,256,2048]{3,2,1,0:T(8,128)(2,1)} %constant_dynamic-slice_fusion.24, pred[]{:T(512)S(6)} %and.21, ...), kind=kOutput, calls=%fused_computation.47.clone.1 | convolution fusion | flops 1110441984 | bytes 9979909 | tf_op jit(solution)/shard_map/while/body/eval_jaxpr/bsd,df->bsf/dot_general | solution.py:432
  71.2 38.4 %all-reduce.7.cloned.1.call-done = f32[1,256,1024]{2,1,0:T(8,128)} async-done(((f32[1,256,1024]{2,1,0:T(8,128)}), f32[1,256,1024]{2,1,0:T(8,128)}) %all-reduce.7.cloned.1.call-update) | async-done | bytes 1048592 | tf_op jit(solution)/shard_map/while/body/eval_jaxpr/psum | solution.py:596
  119.9 8.1 %collective-permute-done = bf16[1,256,1024]{2,1,0:T(8,128)(2,1)} collective-permute-done((bf16[1,256,1024]{2,1,0:T(8,128)(2,1)S(1)}, bf16[1,256,1024]{2,1,0:T(8,128)(2,1)}, u32[]{:S(2)}, u32[]{:S(2)}) %collective-permute-start) | collective-permute-done | bytes 524320 | tf_op jit(solution)/shard_map/while/body/eval_jaxpr/ppermute | solution.py:349
  146.5 9.2 %bitcast_dynamic-update-slice_fusion.10 = (bf16[2,1,256,2048]{3,2,1,0:T(8,128)(2,1)}, bf16[256,2048]{1,0:T(8,128)(2,1)S(1)}, f32[256,2048]{1,0:T(8,128)}) fusion(bf16[2,1,256,2048]{3,2,1,0:T(8,128)(2,1)} %get-tuple-element.2438, s32[]{:T(128)S(6)} %min.21, bf16[1,1,256,2048]{3,2,1,0:T(8,128)(2,1)} %constant_dynamic-slice_fusion.24, pred[]{:T(512)S(6)} %and.21, ...), kind=kOutput, calls=%fused_computation.47.clone.1 | convolution fusion | flops 1110441984 | bytes 9979909 | tf_op jit(solution)/shard_map/while/body/eval_jaxpr/bsd,df->bsf/dot_general | solution.py:432
  171.5 38.4 %all-reduce.7.cloned.1.call-done = f32[1,256,1024]{2,1,0:T(8,128)} async-done(((f32[1,256,1024]{2,1,0:T(8,128)}), f32[1,256,1024]{2,1,0:T(8,128)}) %all-reduce.7.cloned.1.call-update) | async-done | bytes 1048592 | tf_op jit(solution)/shard_map/while/body/eval_jaxpr/psum | solution.py:596
  220.2 8.1 %collective-permute-done = bf16[1,256,1024]{2,1,0:T(8,128)(2,1)} collective-permute-done((bf16[1,256,1024]{2,1,0:T(8,128)(2,1)S(1)}, bf16[1,256,1024]{2,1,0:T(8,128)(2,1)}, u32[]{:S(2)}, u32[]{:S(2)}) %collective-permute-start) | collective-permute-done | bytes 524320 | tf_op jit(solution)/shard_map/while/body/eval_jaxpr/ppermute | solution.py:349
  246.8 9.2 %bitcast_dynamic-update-slice_fusion.10 = (bf16[2,1,256,2048]{3,2,1,0:T(8,128)(2,1)}, bf16[256,2048]{1,0:T(8,128)(2,1)S(1)}, f32[256,2048]{1,0:T(8,128)}) fusion(bf16[2,1,256,2048]{3,2,1,0:T(8,128)(2,1)} %get-tuple-element.2438, s32[]{:T(128)S(6)} %min.21, bf16[1,1,256,2048]{3,2,1,0:T(8,128)(2,1)} %constant_dynamic-slice_fusion.24, pred[]{:T(512)S(6)} %and.21, ...), kind=kOutput, calls=%fused_computation.47.clone.1 | convolution fusion | flops 1110441984 | bytes 9979909 | tf_op jit(solution)/shard_map/while/body/eval_jaxpr/bsd,df->bsf/dot_general | solution.py:432
  271.8 38.4 %all-reduce.7.cloned.1.call-done = f32[1,256,1024]{2,1,0:T(8,128)} async-done(((f32[1,256,1024]{2,1,0:T(8,128)}), f32[1,256,1024]{2,1,0:T(8,128)}) %all-reduce.7.cloned.1.call-update) | async-done | bytes 1048592 | tf_op jit(solution)/shard_map/while/body/eval_jaxpr/psum | solution.py:596
  320.4 8.1 %collective-permute-done = bf16[1,256,1024]{2,1,0:T(8,128)(2,1)} collective-permute-done((bf16[1,256,1024]{2,1,0:T(8,128)(2,1)S(1)}, bf16[1,256,1024]{2,1,0:T(8,128)(2,1)}, u32[]{:S(2)}, u32[]{:S(2)}) %collective-permute-start) | collective-permute-done | bytes 524320 | tf_op jit(solution)/shard_map/while/body/eval_jaxpr/ppermute | solution.py:349
  329.9 256.5 %while.79 = (s32[]{:T(128)}, bf16[1,256,1024]{2,1,0:T(8,128)(2,1)S(1)}, f32[1024]{0:T(1024)S(1)}, f32[1024]{0:T(1024)S(1)}, f32[1024]{0:T(1024)S(1)}, /*index=5*...) while((s32[]{:T(128)}, ...), condition=%wide.region_20.21_spmd.clone, body=%wide.region_7.20_spmd.clone.sunk | while | flops 6822872064 | bytes 193527920 | solution.py:680
  369.5 27.8 %all-reduce.9.cloned.1.call-done = (bf16[1,256,1024]{2,1,0:T(8,128)(2,1)}, bf16[1,256,1024]{2,1,0:T(8,128)(2,1)}) async-done(((bf16[1,256,1024]{2,1,0:T(8,128)(2,1)}, bf16[1,256,1024]{2,1,0:T(8,128)(2,1)}), (bf16[1,256,1024]{2,1,0:T(8,128)(2,1)}, bf16[1,256,1024]{2,1,0:T(8,128)(2,1)})) %all-reduce.9.cloned.1.call-update) | async-done | bytes 1048592 | tf_op jit(solution)/shard_map/while/body/eval_jaxpr/psum | solution.py:640
  402.9 14.8 %collective-permute-done.1 = bf16[1,256,1024]{2,1,0:T(8,128)(2,1)S(1)} collective-permute-done((bf16[1,256,1024]{2,1,0:T(8,128)(2,1)S(1)}, bf16[1,256,1024]{2,1,0:T(8,128)(2,1)S(1)}, u32[]{:S(2)}, u32[]{:S(2)}) %collective-permute-start.1) | collective-permute-done | bytes 524320 | tf_op jit(solution)/shard_map/while/body/eval_jaxpr/ppermute | solution.py:349
  446.4 8.2 %select_add_fusion.28 = f32[2048,1024]{1,0:T(8,128)} fusion(f32[2048,1024]{1,0:T(8,128)} %get-tuple-element.2546, pred[]{:T(512)S(6)} %compare.4, pred[]{:T(512)S(6)} %and.22, bf16[2,1,256,2048]{3,2,1,0:T(8,128)(2,1)S(1)} %copy-done.4, s32[]{:T(128)S(6)} %min.22, bf16[1,256,1024]{2,1,0:T(8,128)(2,1)S(1)} %get-tuple-element.2362), kind=kOutput, calls=%fused_computation.108.clone.1 | convolution fusion | flops 1080033280 | bytes 18350086 | tf_op jit(solution)/shard_map/while/body/eval_jaxpr/bsf,bsd->fd/dot_general | solution.py:488
  459.6 8.1 %select_add_fusion.26 = f32[1024,2048]{1,0:T(8,128)} fusion(f32[1024,2048]{1,0:T(8,128)} %get-tuple-element.2544, bf16[256,2048]{1,0:T(8,128)(2,1)S(1)} %copy-done.12, pred[]{:T(512)S(6)} %compare.4, pred[]{:T(512)S(6)} %and.22, bf16[2,1,256,1024]{3,2,1,0:T(8,128)(2,1)S(1)} %copy-done.10, s32[]{:T(128)S(6)} %min.22), kind=kOutput, calls=%fused_computation.109.clone.1 | convolution fusion | flops 1080033280 | bytes 18350086 | tf_op jit(solution)/shard_map/while/body/eval_jaxpr/bsd,bsf->df/dot_general | solution.py:494
  467.7 13.8 %all-reduce.9.cloned.1.call-done = (bf16[1,256,1024]{2,1,0:T(8,128)(2,1)}, bf16[1,256,1024]{2,1,0:T(8,128)(2,1)}) async-done(((bf16[1,256,1024]{2,1,0:T(8,128)(2,1)}, bf16[1,256,1024]{2,1,0:T(8,128)(2,1)}), (bf16[1,256,1024]{2,1,0:T(8,128)(2,1)}, bf16[1,256,1024]{2,1,0:T(8,128)(2,1)})) %all-reduce.9.cloned.1.call-update) | async-done | bytes 1048592 | tf_op jit(solution)/shard_map/while/body/eval_jaxpr/psum | solution.py:640
  487.1 14.8 %collective-permute-done.1 = bf16[1,256,1024]{2,1,0:T(8,128)(2,1)S(1)} collective-permute-done((bf16[1,256,1024]{2,1,0:T(8,128)(2,1)S(1)}, bf16[1,256,1024]{2,1,0:T(8,128)(2,1)S(1)}, u32[]{:S(2)}, u32[]{:S(2)}) %collective-permute-start.1) | collective-permute-done | bytes 524320 | tf_op jit(solution)/shard_map/while/body/eval_jaxpr/ppermute | solution.py:349
  530.6 8.2 %select_add_fusion.28 = f32[2048,1024]{1,0:T(8,128)} fusion(f32[2048,1024]{1,0:T(8,128)} %get-tuple-element.2546, pred[]{:T(512)S(6)} %compare.4, pred[]{:T(512)S(6)} %and.22, bf16[2,1,256,2048]{3,2,1,0:T(8,128)(2,1)S(1)} %copy-done.4, s32[]{:T(128)S(6)} %min.22, bf16[1,256,1024]{2,1,0:T(8,128)(2,1)S(1)} %get-tuple-element.2362), kind=kOutput, calls=%fused_computation.108.clone.1 | convolution fusion | flops 1080033280 | bytes 18350086 | tf_op jit(solution)/shard_map/while/body/eval_jaxpr/bsf,bsd->fd/dot_general | solution.py:488
  543.8 8.1 %select_add_fusion.26 = f32[1024,2048]{1,0:T(8,128)} fusion(f32[1024,2048]{1,0:T(8,128)} %get-tuple-element.2544, bf16[256,2048]{1,0:T(8,128)(2,1)S(1)} %copy-done.12, pred[]{:T(512)S(6)} %compare.4, pred[]{:T(512)S(6)} %and.22, bf16[2,1,256,1024]{3,2,1,0:T(8,128)(2,1)S(1)} %copy-done.10, s32[]{:T(128)S(6)} %min.22), kind=kOutput, calls=%fused_computation.109.clone.1 | convolution fusion | flops 1080033280 | bytes 18350086 | tf_op jit(solution)/shard_map/while/body/eval_jaxpr/bsd,bsf->df/dot_general | solution.py:494
  551.9 13.8 %all-reduce.9.cloned.1.call-done = (bf16[1,256,1024]{2,1,0:T(8,128)(2,1)}, bf16[1,256,1024]{2,1,0:T(8,128)(2,1)}) async-done(((bf16[1,256,1024]{2,1,0:T(8,128)(2,1)}, bf16[1,256,1024]{2,1,0:T(8,128)(2,1)}), (bf16[1,256,1024]{2,1,0:T(8,128)(2,1)}, bf16[1,256,1024]{2,1,0:T(8,128)(2,1)})) %all-reduce.9.cloned.1.call-update) | async-done | bytes 1048592 | tf_op jit(solution)/shard_map/while/body/eval_jaxpr/psum | solution.py:640
  571.3 14.8 %collective-permute-done.1 = bf16[1,256,1024]{2,1,0:T(8,128)(2,1)S(1)} collective-permute-done((bf16[1,256,1024]{2,1,0:T(8,128)(2,1)S(1)}, bf16[1,256,1024]{2,1,0:T(8,128)(2,1)S(1)}, u32[]{:S(2)}, u32[]{:S(2)}) %collective-permute-start.1) | collective-permute-done | bytes 524320 | tf_op jit(solution)/shard_map/while/body/eval_jaxpr/ppermute | solution.py:349
  609.3 77.5 %shard_map.254 = (bf16[6,2048,512]{2,1,0:T(8,128)(2,1)S(1)}, bf16[32,512]{1,0:T(8,128)(2,1)S(1)}) custom-call(bf16[6,2048,512]{2,1,0:T(8,128)(2,1)S(1)} %copy-done, bf16[32,512]{1,0:T(8,128)(2,1)S(1)} %reshape.1169.small_in), custom_call_target="tpu_custom_call" | custom-call | tf_op jit(solution)/shard_map/pallas_call | solution.py:285
  708.4 12.0 %copy.60 = f32[1024,4,512]{2,1,0:T(4,128)} copy(f32[1024,4,512]{2,0,1:T(8,128)} %convert_bitcast_fusion) | data formatting | bytes 16777216 | tf_op jit(solution)/shard_map/convert_element_type | solution.py:335
  720.4 10.9 %reshape.1173 = f32[1,1024,2048]{2,1,0:T(8,128)} reshape(f32[1024,4,512]{2,1,0:T(4,128)} %copy.60) | data formatting | bytes 16777216 | tf_op jit(solution)/shard_map/convert_element_type | solution.py:335
  (708 shorter events, 317.1 us)
Async XLA Ops:
  27.8 81.8 %all-reduce.7.cloned.1.call-start = ((), (), s32[]{:S(2)}) async-start(), calls=%async_computation | async-start | bytes 2097152 | tf_op jit(solution)/shard_map/while/body/eval_jaxpr/psum | solution.py:596
  69.9 39.7 %copy-start.38 = (f32[1024]{0:T(1024)S(1)}, f32[1024]{0:T(1024)}, u32[]{:S(2)}) copy-start(f32[1024]{0:T(1024)} %copy-done.37) | copy-start | bytes 12292 | tf_op jit(solution)/shard_map/while
  69.9 39.7 %copy-start.40 = (f32[1024]{0:T(1024)S(1)}, f32[1024]{0:T(1024)}, u32[]{:S(2)}) copy-start(f32[1024]{0:T(1024)} %copy-done.39) | copy-start | bytes 12292 | tf_op jit(solution)/shard_map/while
  69.9 39.7 %copy-start.41 = (f32[1024]{0:T(1024)S(1)}, f32[1024]{0:T(1024)}, u32[]{:S(2)}) copy-start(f32[1024]{0:T(1024)} %convert_element_type.711) | copy-start | bytes 12292 | tf_op jit(solution)/shard_map/while
  113.1 14.9 %collective-permute-start = (bf16[1,256,1024]{2,1,0:T(8,128)(2,1)S(1)}, bf16[1,256,1024]{2,1,0:T(8,128)(2,1)}, u32[]{:S(2)}, u32[]{:S(2)}) collective-permute-start(bf16[1,256,1024]{2,1,0:T(8,128)(2,1)S(1)} %get-tuple-element.2314), channel_id=1, source_target_pairs={{0,64},{1,65},{2,66},{3,67},{4,68},{5,69},{6,70},{7,71},{8,72},{9,... | collective-permute-start | bytes 1572872 | tf_op jit(solution)/shard_map/while/body/eval_jaxpr/ppermute | solution.py:349
  128.1 81.8 %all-reduce.7.cloned.1.call-start = ((), (), s32[]{:S(2)}) async-start(), calls=%async_computation | async-start | bytes 2097152 | tf_op jit(solution)/shard_map/while/body/eval_jaxpr/psum | solution.py:596
  170.1 39.7 %copy-start.38 = (f32[1024]{0:T(1024)S(1)}, f32[1024]{0:T(1024)}, u32[]{:S(2)}) copy-start(f32[1024]{0:T(1024)} %copy-done.37) | copy-start | bytes 12292 | tf_op jit(solution)/shard_map/while
  170.1 39.7 %copy-start.40 = (f32[1024]{0:T(1024)S(1)}, f32[1024]{0:T(1024)}, u32[]{:S(2)}) copy-start(f32[1024]{0:T(1024)} %copy-done.39) | copy-start | bytes 12292 | tf_op jit(solution)/shard_map/while
  170.2 39.7 %copy-start.41 = (f32[1024]{0:T(1024)S(1)}, f32[1024]{0:T(1024)}, u32[]{:S(2)}) copy-start(f32[1024]{0:T(1024)} %convert_element_type.711) | copy-start | bytes 12292 | tf_op jit(solution)/shard_map/while
  170.2 39.7 %copy-start.42 = (f32[1024]{0:T(1024)S(1)}, f32[1024]{0:T(1024)}, u32[]{:S(2)}) copy-start(f32[1024]{0:T(1024)} %convert_element_type.712) | copy-start | bytes 12292 | tf_op jit(solution)/shard_map/while
  170.2 39.7 %copy-start.45 = (f32[1024]{0:T(1024)S(1)}, f32[1024]{0:T(1024)}, u32[]{:S(2)}) copy-start(f32[1024]{0:T(1024)} %get-tuple-element.2490) | copy-start | bytes 12292 | tf_op jit(solution)/shard_map/while
  213.4 14.9 %collective-permute-start = (bf16[1,256,1024]{2,1,0:T(8,128)(2,1)S(1)}, bf16[1,256,1024]{2,1,0:T(8,128)(2,1)}, u32[]{:S(2)}, u32[]{:S(2)}) collective-permute-start(bf16[1,256,1024]{2,1,0:T(8,128)(2,1)S(1)} %get-tuple-element.2314), channel_id=1, source_target_pairs={{0,64},{1,65},{2,66},{3,67},{4,68},{5,69},{6,70},{7,71},{8,72},{9,... | collective-permute-start | bytes 1572872 | tf_op jit(solution)/shard_map/while/body/eval_jaxpr/ppermute | solution.py:349
  228.4 81.8 %all-reduce.7.cloned.1.call-start = ((), (), s32[]{:S(2)}) async-start(), calls=%async_computation | async-start | bytes 2097152 | tf_op jit(solution)/shard_map/while/body/eval_jaxpr/psum | solution.py:596
  270.4 39.7 %copy-start.38 = (f32[1024]{0:T(1024)S(1)}, f32[1024]{0:T(1024)}, u32[]{:S(2)}) copy-start(f32[1024]{0:T(1024)} %copy-done.37) | copy-start | bytes 12292 | tf_op jit(solution)/shard_map/while
  270.4 39.7 %copy-start.40 = (f32[1024]{0:T(1024)S(1)}, f32[1024]{0:T(1024)}, u32[]{:S(2)}) copy-start(f32[1024]{0:T(1024)} %copy-done.39) | copy-start | bytes 12292 | tf_op jit(solution)/shard_map/while
  270.4 39.7 %copy-start.41 = (f32[1024]{0:T(1024)S(1)}, f32[1024]{0:T(1024)}, u32[]{:S(2)}) copy-start(f32[1024]{0:T(1024)} %convert_element_type.711) | copy-start | bytes 12292 | tf_op jit(solution)/shard_map/while
  270.5 39.7 %copy-start.42 = (f32[1024]{0:T(1024)S(1)}, f32[1024]{0:T(1024)}, u32[]{:S(2)}) copy-start(f32[1024]{0:T(1024)} %convert_element_type.712) | copy-start | bytes 12292 | tf_op jit(solution)/shard_map/while
  313.6 14.9 %collective-permute-start = (bf16[1,256,1024]{2,1,0:T(8,128)(2,1)S(1)}, bf16[1,256,1024]{2,1,0:T(8,128)(2,1)}, u32[]{:S(2)}, u32[]{:S(2)}) collective-permute-start(bf16[1,256,1024]{2,1,0:T(8,128)(2,1)S(1)} %get-tuple-element.2314), channel_id=1, source_target_pairs={{0,64},{1,65},{2,66},{3,67},{4,68},{5,69},{6,70},{7,71},{8,72},{9,... | collective-permute-start | bytes 1572872 | tf_op jit(solution)/shard_map/while/body/eval_jaxpr/ppermute | solution.py:349
  330.0 67.3 %all-reduce.9.cloned.1.call-start = ((), (), s32[]{:S(2)}) async-start(), calls=%async_computation.1 | async-start | bytes 2097152 | tf_op jit(solution)/shard_map/while/body/eval_jaxpr/psum | solution.py:640
  401.6 16.2 %collective-permute-start.1 = (bf16[1,256,1024]{2,1,0:T(8,128)(2,1)S(1)}, bf16[1,256,1024]{2,1,0:T(8,128)(2,1)S(1)}, u32[]{:S(2)}, u32[]{:S(2)}) collective-permute-start(bf16[1,256,1024]{2,1,0:T(8,128)(2,1)S(1)} %get-tuple-element.2380), channel_id=1, source_target_pairs={{64,0},{65,1},{66,2},{67,3},{68,4},{69,5},{70,6},{71,7},{72,8},{73... | collective-permute-start | bytes 1572872 | tf_op jit(solution)/shard_map/while/body/eval_jaxpr/ppermute | solution.py:349
  417.8 63.7 %all-reduce.9.cloned.1.call-start = ((), (), s32[]{:S(2)}) async-start(), calls=%async_computation.1 | async-start | bytes 2097152 | tf_op jit(solution)/shard_map/while/body/eval_jaxpr/psum | solution.py:640
  485.8 16.2 %collective-permute-start.1 = (bf16[1,256,1024]{2,1,0:T(8,128)(2,1)S(1)}, bf16[1,256,1024]{2,1,0:T(8,128)(2,1)S(1)}, u32[]{:S(2)}, u32[]{:S(2)}) collective-permute-start(bf16[1,256,1024]{2,1,0:T(8,128)(2,1)S(1)} %get-tuple-element.2380), channel_id=1, source_target_pairs={{64,0},{65,1},{66,2},{67,3},{68,4},{69,5},{70,6},{71,7},{72,8},{73... | collective-permute-start | bytes 1572872 | tf_op jit(solution)/shard_map/while/body/eval_jaxpr/ppermute | solution.py:349
  502.0 63.7 %all-reduce.9.cloned.1.call-start = ((), (), s32[]{:S(2)}) async-start(), calls=%async_computation.1 | async-start | bytes 2097152 | tf_op jit(solution)/shard_map/while/body/eval_jaxpr/psum | solution.py:640
  570.0 16.2 %collective-permute-start.1 = (bf16[1,256,1024]{2,1,0:T(8,128)(2,1)S(1)}, bf16[1,256,1024]{2,1,0:T(8,128)(2,1)S(1)}, u32[]{:S(2)}, u32[]{:S(2)}) collective-permute-start(bf16[1,256,1024]{2,1,0:T(8,128)(2,1)S(1)} %get-tuple-element.2380), channel_id=1, source_target_pairs={{64,0},{65,1},{66,2},{67,3},{68,4},{69,5},{70,6},{71,7},{72,8},{73... | collective-permute-start | bytes 1572872 | tf_op jit(solution)/shard_map/while/body/eval_jaxpr/ppermute | solution.py:349
  (165 other events, 1001.8 us)
Sparse Core Ops, SparseCore 0:
  59.5 50.0 all-reduce.6
  159.8 50.0 all-reduce.6
  260.1 50.0 all-reduce.6
  347.2 50.0 all-reduce.8
  434.9 46.5 all-reduce.8
  519.1 46.5 all-reduce.8
